TPU v7x, 32 devices: a whole 2x2x4 slice. The times are simulated.
32 devices in a mesh: gx: 4 (over z), gy: 4 (over y, x), gz: 2 (over core).
Axes of the slice: x: 2, y: 2, z: 4, core: 2. Of those that a mesh axis runs over, the one named last changes fastest.
Arguments:
- moment: bfloat16 [1024, 1024, 1024], P('gx', 'gy', 'gz'), may hold values from -0.625 to 0.625
- factor_start: bfloat16 [1024, 128], replicated, may hold values from -6 to 6
Outputs:
- factor_out: float32 [1024, 128], P('gx')
All inputs are finite; a program needn't handle non-finite values.
Results may differ from a plain program's by a relative error of at most 0.0005.
Values may be sent and summed in bfloat16 or wider, within the bound.
A program may use at most 128 MiB of HBM per device.

v0:
```python
import jax
import jax.numpy as jnp
from jax import lax
from jax.sharding import PartitionSpec as P


def local(moment, factor_start):
    rows_i, rows_j, rows_k = moment.shape
    order, rank = factor_start.shape
    idx_x = lax.axis_index("gx")
    idx_z = lax.axis_index("gz")
    scale_n = 1.0 / order**0.5
    krows = lax.dynamic_slice_in_dim(factor_start, idx_z * rows_k, rows_k, 0)
    partial_y = jnp.einsum("ijk,kb->ijb", moment, krows, preferred_element_type=jnp.float32)
    ysum = lax.psum_scatter(partial_y.astype(jnp.bfloat16), "gz", scatter_dimension=2, tiled=True)
    row_start = idx_x * rows_i
    out = jnp.einsum(
        "ijb,ja->iba",
        lax.all_to_all(ysum, "gy", split_axis=2, concat_axis=1, tiled=True),
        factor_start,
        preferred_element_type=jnp.float32,
    )
    ztens = (out * scale_n).astype(jnp.bfloat16)
    here_rows = ztens.shape[0]
    irows = lax.dynamic_slice_in_dim(factor_start, row_start, here_rows, 0)
    cpart = jnp.einsum("iba,ir->bar", ztens, irows, preferred_element_type=jnp.float32)
    csum = lax.psum(cpart, "gx")
    cgram = (csum * scale_n).astype(jnp.bfloat16)
    vpart = jnp.einsum("iba,bar->ir", ztens, cgram, preferred_element_type=jnp.float32)
    vnew = lax.psum(vpart, ("gy", "gz")) / rank
    total = lax.psum(jnp.sum(vnew * vnew), "gx")
    scaled = vnew * lax.rsqrt(total / (order * rank) + 1e-06)
    return scaled


def solution(mesh):
    in_specs = (P("gx", "gy", "gz"), P())
    out_specs = P("gx", None)
    return jax.shard_map(local, mesh=mesh, in_specs=in_specs, out_specs=out_specs, check_vma=False)
```

profile of v0, /device:TPU:0, one launch (start us, length us, event | category | flops | bytes accessed | tf_op | source)
XLA Modules:
  0.0 343.0 jit_solution(15025529840757331126)
XLA Ops:
  6.5 0.0 copy-start
  6.5 0.0 reduce-scatter.2.cloned.1.call-start
  6.5 0.9 copy-done
  7.5 33.3 %convert_bitcast_fusion = bf16[256,256,128]{1,2,0:T(8,128)(2,1)} fusion(bf16[256,256,512]{2,1,0:T(8,128)(2,1)} %param.2, bf16[1024,128]{1,0:T(8,128)(2,1)S(1)} %copy-done, s32[]{:T(128)S(6)} %select_n.6), kind=kOutput, calls=%fused_computation | convolution fusion | flops 8598323200 | bytes 84017152 | tf_op jit(solution)/shard_map/ijk,kb->ijb/dot_general | solution.py:14
  40.8 0.0 reduce-scatter.2.cloned.1.call-update
  40.8 29.1 %reduce-scatter.2.cloned.1.call-done = bf16[256,256,64]{1,2,0:T(8,128)(2,1)} async-done(((bf16[256,256,128]{1,2,0:T(8,128)(2,1)}), bf16[256,256,64]{1,2,0:T(8,128)(2,1)}) %reduce-scatter.2.cloned.1.call-update) | async-done | bytes 8388624 | tf_op jit(solution)/shard_map/reduce_scatter | solution.py:15
  70.0 11.4 %copy.6 = bf16[256,256,64]{1,0,2:T(8,128)(2,1)} copy(bf16[256,256,64]{1,2,0:T(8,128)(2,1)} %reduce-scatter.2.cloned.1.call-done) | data formatting | bytes 16777216 | tf_op jit(solution)/shard_map/reduce_scatter | solution.py:15
  81.3 5.7 %all-to-all-start = ((bf16[256,256,64]{1,0,2:T(8,128)(2,1)}), bf16[256,256,64]{1,0,2:T(8,128)(2,1)}, u32[]{:S(2)}, u32[]{:S(2)}) async-start(bf16[256,256,64]{1,0,2:T(8,128)(2,1)} %copy.6), calls=%async_computation.1 | async-start | bytes 16777216 | tf_op jit(solution)/shard_map/all_to_all | solution.py:19
  87.0 0.2 all-reduce.3.cloned.1.call-start
  87.2 92.8 %all-to-all-done = bf16[256,256,64]{1,0,2:T(8,128)(2,1)} async-done(((bf16[256,256,64]{1,0,2:T(8,128)(2,1)}), bf16[256,256,64]{1,0,2:T(8,128)(2,1)}, u32[]{:S(2)}, u32[]{:S(2)}) %all-to-all-start) | async-done | bytes 8388640 | tf_op jit(solution)/shard_map/all_to_all | solution.py:19
  180.1 11.1 %copy.10 = bf16[256,256,4,16]{1,2,0,3:T(4,128)(2,1)} copy(bf16[256,256,4,16]{1,0,3,2:T(8,128)(2,1)} %bitcast.2) | data formatting | bytes 16777216 | tf_op jit(solution)/shard_map/all_to_all | solution.py:19
  191.1 14.3 %all_to_all.16 = bf16[256,1024,16]{1,0,2:T(8,128)(2,1)} reshape(bf16[256,4,256,16]{2,1,0,3:T(4,128)(2,1)} %bitcast.24) | data formatting | bytes 16777216 | tf_op jit(solution)/shard_map/all_to_all | solution.py:19
  205.4 5.7 %multiply_convert_fusion = bf16[256,16,128]{2,0,1:T(8,128)(2,1)S(1)} fusion(bf16[256,1024,16]{1,0,2:T(8,128)(2,1)} %all_to_all.16, bf16[1024,128]{1,0:T(8,128)(2,1)S(1)} %copy-done), kind=kOutput, calls=%fused_computation.2 | convolution fusion | flops 1074790400 | bytes 9699328 | tf_op jit(solution)/shard_map/ijb,ja->iba/dot_general | solution.py:17
  211.1 1.5 fusion.4
  212.7 0.0 all-reduce.3.cloned.1.call-update
  212.7 0.0 all-reduce.5.cloned.1.call-start
  212.7 52.2 %all-reduce.3.cloned.1.call-done = f32[16,128,128]{2,1,0:T(8,128)} async-done(((f32[16,128,128]{2,1,0:T(8,128)}), f32[16,128,128]{2,1,0:T(8,128)}) %all-reduce.3.cloned.1.call-update) | async-done | bytes 1048592 | tf_op jit(solution)/shard_map/psum | solution.py:27
  264.9 2.3 convolution_bitcast_fusion
  267.2 0.0 all-reduce.5.cloned.1.call-update
  267.3 53.1 %all-reduce.5.cloned.1.call-done = f32[256,128]{1,0:T(8,128)} async-done(((f32[256,128]{1,0:T(8,128)}), f32[256,128]{1,0:T(8,128)}) %all-reduce.5.cloned.1.call-update) | async-done | bytes 131088 | tf_op jit(solution)/shard_map/psum | solution.py:30
  320.3 1.5 multiply_reduce_fusion
  321.9 12.3 %psum.23 = f32[]{:T(128)} all-reduce(f32[]{:T(128)} %multiply_reduce_fusion), channel_id=1, replica_groups=mesh['gx'=4,'gy'=4,'gz'=2] {'gx'}, use_global_device_ids=true, to_apply=%region_4.0 | all-reduce | flops 1 | bytes 8 | tf_op jit(solution)/shard_map/psum | solution.py:31
  334.9 1.6 broadcast_multiply_fusion
Async XLA Ops:
  6.5 1.0 copy-start
  6.5 63.4 %reduce-scatter.2.cloned.1.call-start = ((), (), s32[]{:S(2)}) async-start(), calls=%async_computation.2 | async-start | bytes 25165824 | tf_op jit(solution)/shard_map/reduce_scatter | solution.py:15
  81.3 98.7 %all-to-all-start = ((bf16[256,256,64]{1,0,2:T(8,128)(2,1)}), bf16[256,256,64]{1,0,2:T(8,128)(2,1)}, u32[]{:S(2)}, u32[]{:S(2)}) async-start(bf16[256,256,64]{1,0,2:T(8,128)(2,1)} %copy.6), calls=%async_computation.1 | async-start | bytes 16777216 | tf_op jit(solution)/shard_map/all_to_all | solution.py:19
  87.0 177.9 %all-reduce.3.cloned.1.call-start = ((), (), s32[]{:S(2)}) async-start(), calls=%async_computation.3 | async-start | bytes 2097152 | tf_op jit(solution)/shard_map/psum | solution.py:27
  212.7 107.6 %all-reduce.5.cloned.1.call-start = ((), (), s32[]{:S(2)}) async-start(), calls=%async_computation.4 | async-start | bytes 262144 | tf_op jit(solution)/shard_map/psum | solution.py:30
Sparse Core Ops, SparseCore 0:
  40.9 28.9 reduce-scatter.1
  212.8 52.0 all-reduce.2
  268.0 52.3 all-reduce.4
where the time goes:
time: 344 us; the launch traced here: 343 us
  waiting for transfers between devices  227 us (66%)
  matrix products  42.9 us (12%)
  local copies, waits for them, and re-layouts  37.7 us (11%)
  between operations  13.8 us (4%)
  blocking collectives  12.3 us (4%)
  starting transfers between devices  5.92 us (2%)
    all_to_all x1, waiting for transfers between devices, local(): lax.all_to_all(ysum, 'gy', split_axis=2, concat_axis=1, tiled=True)  92.8 us
    psum x1, waiting for transfers between devices, local(): vnew = lax.psum(vpart, ('gy', 'gz')) / rank  53.1 us
    psum x1, waiting for transfers between devices, local(): csum = lax.psum(cpart, 'gx')  52.2 us
    dot_general x1, matrix products, local(): jnp.einsum('ijk,kb->ijb', moment, krows, preferred_element_type=jnp.float32)  33.3 us
    reduce_scatter x1, waiting for transfers between devices, local(): lax.psum_scatter(partial_y.astype(jnp.bfloat16), 'gz', scatter_dimension=...  29.1 us
    all_to_all x2, local copies, waits for them, and re-layouts, local(): lax.all_to_all(ysum, 'gy', split_axis=2, concat_axis=1, tiled=True)  25.3 us
    psum x1, blocking collectives, local(): total = lax.psum(jnp.sum(vnew * vnew), 'gx')  12.3 us
    reduce_scatter x1, local copies, waits for them, and re-layouts, local(): lax.psum_scatter(partial_y.astype(jnp.bfloat16), 'gz', scatter_dimension=...  11.4 us
  transfers between devices with their start and end apart: 4, of which 4 were waited for; matrix products, arithmetic and copies ran while one was open for 0% of the time, Pallas kernels for 0%

commit v1 on v0

v1 whole, which is shorter than its diff:
```python
import functools

import jax
import jax.numpy as jnp
from jax import lax
from jax.experimental import pallas as pl
from jax.experimental.pallas import tpu as pltpu
from jax.sharding import PartitionSpec as P

MESH = pl.DeviceIdType.MESH
F32 = jnp.float32
BF16 = jnp.bfloat16
STEP_ROWS = 16
MBUFS = 4
PIECES = 4


def sweep_kernel(nx, order, m_hbm, u_ref, out_ref, mbuf, uj_t, ui_t, zf, zsend, prx, kept, xs, rx, zz,
                 cs, crx, cown, lsend, r1, r2, cfull, vs, vrx, vfull, ss, ssrx,
                 m_sem, p_send, p_recv, x_send, x_recv, y_send, y_recv, c_send, c_recv, l_send, r1_recv, r2_recv,
                 o_send, g_send, g_recv, v_send, v_recv, f_send, f_recv, s_send, s_recv):
    rows_i, rows_j, rows_k = m_hbm.shape
    rank = u_ref.shape[1]
    steps = rows_i // STEP_ROWS
    scale = 1.0 / order**0.5
    me_x, me_y, me_c = lax.axis_index("gx"), lax.axis_index("gy"), lax.axis_index("gz")
    bit_x, bit_y = lax.rem(me_y, 2), lax.div(me_y, 2)
    at_x = (me_x, me_y + 1 - 2 * bit_x, me_c)
    at_y = (me_x, me_y + 2 - 4 * bit_y, me_c)
    at_c = (me_x, me_y, 1 - me_c)
    me_e = me_y * 2 + me_c
    half = rank // 2
    quarter = rank // 4
    part = rank // 8
    sub = rank // 16
    piece = sub // 2

    def group(d):
        e = lax.rem(me_e + d, 8)
        return e, (me_x, lax.div(e, 2), lax.rem(e, 2))

    def line(d):
        return (lax.rem(me_x + d, nx), me_y, me_c)

    def m_copy(t):
        slot = lax.rem(t, MBUFS)
        return pltpu.make_async_copy(m_hbm.at[pl.ds(t * STEP_ROWS, STEP_ROWS)], mbuf.at[slot], m_sem.at[slot])

    def remote(src, dst, send, recv, to):
        return pltpu.make_async_remote_copy(src_ref=src, dst_ref=dst, send_sem=send, recv_sem=recv,
                                            device_id=to, device_id_type=MESH)

    for t in range(MBUFS - 1):
        m_copy(t).start()

    barrier = pltpu.get_barrier_semaphore()
    for d in range(1, 8):
        pl.semaphore_signal(barrier, inc=1, device_id=group(d)[1], device_id_type=MESH)
    for d in range(1, nx):
        pl.semaphore_signal(barrier, inc=1, device_id=line(d), device_id_type=MESH)

    uj_t[...] = u_ref[pl.ds(me_y * rows_j, rows_j), :].astype(F32).T.astype(BF16)
    ui_t[...] = u_ref[pl.ds(me_x * rows_i, rows_i), :].astype(F32).T.astype(BF16)
    pl.semaphore_wait(barrier, 7 + nx - 1)

    def p_copy(t):
        return remote(zsend.at[t], prx.at[t], p_send.at[t], p_recv.at[t], at_c)

    def x_copy(t):
        return remote(xs.at[t, pl.ds(0, part)], rx.at[t, pl.ds(0, part)], x_send.at[t], x_recv.at[t], at_x)

    def y_copy(t):
        return remote(xs.at[t, pl.ds(part, part)], rx.at[t, pl.ds(part, part)], y_send.at[t], y_recv.at[t], at_y)

    def contract(t):
        par = lax.rem(t, 2)
        m_copy(t).wait()
        block = mbuf[lax.rem(t, MBUFS)].reshape(STEP_ROWS * rows_j, rows_k)
        uk = u_ref[pl.ds(me_c * rows_k, rows_k), :]
        y = jnp.dot(block, uk, preferred_element_type=F32).astype(BF16)
        for i in range(0, STEP_ROWS, 2):
            pair = jnp.concatenate([y[i * rows_j:(i + 1) * rows_j], y[(i + 1) * rows_j:(i + 2) * rows_j]], axis=1)
            z = jnp.dot(uj_t[...], pair, preferred_element_type=F32) * scale
            zf[par, pl.ds(i, rank, stride=STEP_ROWS), :] = z[:, :rank]
            zf[par, pl.ds(i + 1, rank, stride=STEP_ROWS), :] = z[:, rank:]
        other = zf[par, pl.ds((1 - me_c) * half * STEP_ROWS, half * STEP_ROWS), :]
        zsend[t] = other.astype(BF16).reshape(half, STEP_ROWS, rank)
        p_copy(t).start()

    def pair_sum(t):
        par = lax.rem(t, 2)
        p_copy(t).wait_recv()

        def summed(first):
            mine = zf[par, pl.ds((me_c * half + first) * STEP_ROWS, part * STEP_ROWS), :]
            return mine.reshape(part, STEP_ROWS, rank) + prx[t, pl.ds(first, part)].astype(F32)

        xs[t, pl.ds(0, part)] = summed((1 - bit_x) * part).astype(BF16)
        x_copy(t).start()
        xs[t, pl.ds(part, part)] = summed(quarter + (1 - bit_y) * part).astype(BF16)
        y_copy(t).start()
        kept[t, pl.ds(0, part)] = summed(bit_x * part)
        kept[t, pl.ds(part, part)] = summed(quarter + bit_y * part)

    contract(0)

    def body(t, carry):
        @pl.when(t + MBUFS - 2 < steps)
        def _():
            m_copy(t + MBUFS - 2).start()

        pair_sum(t - 1)
        contract(t)
        return carry

    lax.fori_loop(1, steps, body, 0)
    pair_sum(steps - 1)

    def landed(t, carry):
        x_copy(t).wait_recv()
        y_copy(t).wait_recv()
        return carry

    lax.fori_loop(0, steps, landed, 0)

    def total_z(a, carry):
        zz[a] = (kept[:, a] + rx[:, a].astype(F32)).astype(BF16).reshape(rows_i, rank)
        return carry

    lax.fori_loop(0, 2 * part, total_z, 0)

    def first_of(k, mine):
        if k % 2 == 0:
            bit = bit_y if mine else 1 - bit_y
            return bit * sub + (k // 2) * piece
        bit = bit_x if mine else 1 - bit_x
        return part + bit * sub + (k // 2) * piece

    def wide_z(first):
        return jnp.concatenate([zz[first + n] for n in range(piece)], axis=1)

    def core_part(first):
        return jnp.dot(ui_t[...], wide_z(first), preferred_element_type=F32) * scale

    def c_copy(k):
        return remote(cs.at[k], crx.at[k], c_send.at[k], c_recv.at[k], at_y if k % 2 == 0 else at_x)

    for k in range(PIECES):
        c = core_part(first_of(k, False))
        for n in range(piece):
            cs[k, n] = c[:, n * rank:(n + 1) * rank].astype(BF16)
        c_copy(k).start()
    for k in range(PIECES):
        c = core_part(first_of(k, True))
        for n in range(piece):
            cown[k, n] = c[:, n * rank:(n + 1) * rank]

    mid = nx // 2
    side = lax.div(me_x, mid)
    inward = (me_x + 1 - 2 * side, me_y, me_c)
    outward = (me_x - 1 + 2 * side, me_y, me_c)
    inner = jnp.logical_or(me_x == mid - 1, me_x == mid)
    has_out = jnp.logical_and(me_x > 0, me_x < nx - 1)
    not_inner = jnp.logical_not(inner)

    def l1_copy(k):
        return remote(lsend.at[k], r1.at[k], l_send.at[k], r1_recv.at[k], inward)

    def l2_copy(k):
        return remote(lsend.at[k], r2.at[k], l_send.at[k], r2_recv.at[k], inward)

    def o_copy(k):
        return remote(cfull.at[pl.ds(first_of(k, True), piece)], r2.at[k], o_send.at[k], r2_recv.at[k], outward)

    def g_copy(k):
        here = cfull.at[pl.ds(first_of(k, True), piece)]
        return remote(here, here, g_send.at[k], g_recv.at[k], at_y if k % 2 == 0 else at_x)

    def g_landed(k):
        here = cfull.at[pl.ds(first_of(k, False), piece)]
        return remote(here, here, g_send.at[k], g_recv.at[k], at_y if k % 2 == 0 else at_x)

    for k in range(PIECES):
        c_copy(k).wait_recv()
        cown[k] = cown[k] + crx[k].astype(F32)

        @pl.when(has_out)
        def _():
            l1_copy(k).wait_recv()
            cown[k] = cown[k] + r1[k].astype(F32)

        lsend[k] = cown[k].astype(BF16)

        @pl.when(inner)
        def _():
            l2_copy(k).start()

        @pl.when(not_inner)
        def _():
            l1_copy(k).start()

    def v_part(first):
        c = jnp.concatenate([cfull[first + n] for n in range(piece)], axis=1)
        return lax.dot_general(wide_z(first), c, (((1,), (1,)), ((), ())), preferred_element_type=F32)

    for k in range(PIECES):
        l2_copy(k).wait_recv()
        first = first_of(k, True)

        @pl.when(inner)
        def _():
            cfull[pl.ds(first, piece)] = (lsend[k].astype(F32) + r2[k].astype(F32)).astype(BF16)

        @pl.when(not_inner)
        def _():
            cfull[pl.ds(first, piece)] = r2[k]

        @pl.when(has_out)
        def _():
            o_copy(k).start()

        g_copy(k).start()
        if k == 0:
            vs[...] = v_part(first)
        else:
            vs[...] = vs[...] + v_part(first)
    for k in range(PIECES):
        g_landed(k).wait_recv()
        vs[...] = vs[...] + v_part(first_of(k, False))

    vrows = rows_i // 8

    def v_copy(d):
        e, to = group(d)
        return remote(vs.at[pl.ds(e * vrows, vrows)], vrx.at[d - 1], v_send.at[d - 1], v_recv.at[d - 1], to)

    def f_copy(d):
        here = vfull.at[pl.ds(me_e * vrows, vrows)]
        return remote(here, here, f_send.at[d - 1], f_recv.at[d - 1], group(d)[1])

    def f_landed(d):
        here = vfull.at[pl.ds(group(8 - d)[0] * vrows, vrows)]
        return remote(here, here, f_send.at[d - 1], f_recv.at[d - 1], group(d)[1])

    def s_copy(d):
        return remote(ss, ssrx.at[d - 1], s_send.at[d - 1], s_recv.at[d - 1], line(d))

    for d in range(1, 8):
        v_copy(d).start()
    total = vs[pl.ds(me_e * vrows, vrows), :]
    for d in range(1, 8):
        v_copy(d).wait_recv()
        total = total + vrx[d - 1]
    vfull[pl.ds(me_e * vrows, vrows), :] = total * (1.0 / rank)
    for d in range(1, 8):
        f_copy(d).start()
    for d in range(1, 8):
        f_landed(d).wait_recv()
    vnew = vfull[...]
    ss[...] = jnp.sum((vnew * vnew).reshape(rows_i // 8, 8, rank), axis=0)
    for d in range(1, nx):
        s_copy(d).start()
    square = ss[...]
    for d in range(1, nx):
        s_copy(d).wait_recv()
        square = square + ssrx[d - 1]
    square = jnp.sum(jnp.sum(square, axis=0, keepdims=True), axis=1, keepdims=True)
    out_ref[...] = vnew * lax.rsqrt(square / (order * rank) + 1e-06)

    def sent(t, carry):
        p_copy(t).wait_send()
        x_copy(t).wait_send()
        y_copy(t).wait_send()
        return carry

    lax.fori_loop(0, steps, sent, 0)
    for k in range(PIECES):
        c_copy(k).wait_send()
        l2_copy(k).wait_send()
        g_copy(k).wait_send()

        @pl.when(has_out)
        def _():
            o_copy(k).wait_send()
    for d in range(1, 8):
        v_copy(d).wait_send()
        f_copy(d).wait_send()
    for d in range(1, nx):
        s_copy(d).wait_send()


def fused(nx, moment, factor_start):
    rows_i, rows_j, rows_k = moment.shape
    order, rank = factor_start.shape
    steps = rows_i // STEP_ROWS
    half, part, piece = rank // 2, rank // 8, rank // 32
    vrows = rows_i // 8
    vmem, dma = pltpu.VMEM, pltpu.SemaphoreType.DMA
    scratch = [
        vmem((MBUFS, STEP_ROWS, rows_j, rows_k), BF16),
        vmem((rank, rows_j), BF16),
        vmem((rank, rows_i), BF16),
        vmem((2, rank * STEP_ROWS, rank), F32),
        vmem((steps, half, STEP_ROWS, rank), BF16),
        vmem((steps, half, STEP_ROWS, rank), BF16),
        vmem((steps, 2 * part, STEP_ROWS, rank), F32),
        vmem((steps, 2 * part, STEP_ROWS, rank), BF16),
        vmem((steps, 2 * part, STEP_ROWS, rank), BF16),
        vmem((2 * part, rows_i, rank), BF16),
        vmem((PIECES, piece, rank, rank), BF16),
        vmem((PIECES, piece, rank, rank), BF16),
        vmem((PIECES, piece, rank, rank), F32),
        vmem((PIECES, piece, rank, rank), BF16),
        vmem((PIECES, piece, rank, rank), BF16),
        vmem((PIECES, piece, rank, rank), BF16),
        vmem((2 * part, rank, rank), BF16),
        vmem((rows_i, rank), F32),
        vmem((7, vrows, rank), F32),
        vmem((rows_i, rank), F32),
        vmem((8, rank), F32),
        vmem((nx - 1, 8, rank), F32),
        dma((MBUFS,)),
        dma((steps,)), dma((steps,)), dma((steps,)), dma((steps,)), dma((steps,)), dma((steps,)),
        dma((PIECES,)), dma((PIECES,)), dma((PIECES,)), dma((PIECES,)), dma((PIECES,)),
        dma((PIECES,)), dma((PIECES,)), dma((PIECES,)),
        dma((7,)), dma((7,)), dma((7,)), dma((7,)),
        dma((nx - 1,)), dma((nx - 1,)),
    ]
    return pl.pallas_call(
        functools.partial(sweep_kernel, nx, order),
        out_shape=jax.ShapeDtypeStruct((rows_i, rank), F32),
        in_specs=[pl.BlockSpec(memory_space=pl.ANY), pl.BlockSpec(memory_space=pltpu.VMEM)],
        out_specs=pl.BlockSpec(memory_space=pltpu.VMEM),
        scratch_shapes=scratch,
        compiler_params=pltpu.CompilerParams(collective_id=0, has_side_effects=True,
                                             vmem_limit_bytes=60 * 1024 * 1024),
        cost_estimate=pl.CostEstimate(flops=2 * rows_i * rows_j * rank * (rows_k + rank),
                                      bytes_accessed=2 * rows_i * rows_j * rows_k, transcendentals=0),
    )(moment, factor_start)


def plain(moment, factor_start):
    rows_i, rows_j, rows_k = moment.shape
    order, rank = factor_start.shape
    scale = 1.0 / order**0.5
    krows = lax.dynamic_slice_in_dim(factor_start, lax.axis_index("gz") * rows_k, rows_k, 0)
    jrows = lax.dynamic_slice_in_dim(factor_start, lax.axis_index("gy") * rows_j, rows_j, 0)
    irows = lax.dynamic_slice_in_dim(factor_start, lax.axis_index("gx") * rows_i, rows_i, 0)
    y = jnp.einsum("ijk,kb->ijb", moment, krows, preferred_element_type=F32).astype(BF16)
    z = jnp.einsum("ijb,ja->iba", y, jrows, preferred_element_type=F32) * scale
    z = lax.psum_scatter(z, "gz", scatter_dimension=1, tiled=True)
    z = lax.psum_scatter(z, "gy", scatter_dimension=2, tiled=True).astype(BF16)
    c = lax.psum(jnp.einsum("iba,ir->bar", z, irows, preferred_element_type=F32), "gx")
    c = (c * scale).astype(BF16)
    v = lax.psum(jnp.einsum("iba,bar->ir", z, c, preferred_element_type=F32), ("gy", "gz")) / rank
    total = lax.psum(jnp.sum(v * v), "gx")
    return v * lax.rsqrt(total / (order * rank) + 1e-06)


def solution(mesh):
    nx, ny, nz = mesh.shape["gx"], mesh.shape["gy"], mesh.shape["gz"]

    def local(moment, factor_start):
        rows_i, rank = moment.shape[0], factor_start.shape[1]
        if ny == 4 and nz == 2 and nx % 2 == 0 and rank == 128 and rows_i % 128 == 0:
            return fused(nx, moment, factor_start)
        return plain(moment, factor_start)

    return jax.shard_map(local, mesh=mesh, in_specs=(P("gx", "gy", "gz"), P()), out_specs=P("gx", None),
                         check_vma=False)
```

time: 344 us -> 105 us (0.31)
  waiting for transfers between devices: 227 us -> 0 us
  Pallas kernels: 0 us -> 103 us
  matrix products: 42.9 us -> 0 us
  local copies, waits for them, and re-layouts: 37.7 us -> 1.57 us
  between operations: 13.8 us -> 0.01 us
  blocking collectives: 12.3 us -> 0 us
  starting transfers between devices: 5.92 us -> 0 us
    psum x2 -> x0, waiting for transfers between devices: 105 us -> none  [the longest x1 53.1 us: local(): vnew = lax.psum(vpart, ('gy', 'gz')) / rank]
    pallas_call x0 -> x1, Pallas kernels: none -> 103 us  [fused(): pl.pallas_call(functools.partial(sweep_kernel, nx, order), out_shape=jax....]
    all_to_all x1 -> x0, waiting for transfers between devices: 92.8 us -> none  [local(): lax.all_to_all(ysum, 'gy', split_axis=2, concat_axis=1, tiled=True)]
    dot_general x4 -> x0, matrix products: 42.9 us -> none  [the longest x1 33.3 us: local(): jnp.einsum('ijk,kb->ijb', moment, krows, preferred_element_type=jnp.float32)]
    reduce_scatter x1 -> x0, waiting for transfers between devices: 29.1 us -> none  [local(): lax.psum_scatter(partial_y.astype(jnp.bfloat16), 'gz', scatter_dimension=...]
    all_to_all x2 -> x0, local copies, waits for them, and re-layouts: 25.3 us -> none  [local(): lax.all_to_all(ysum, 'gy', split_axis=2, concat_axis=1, tiled=True)]
    psum x1 -> x0, blocking collectives: 12.3 us -> none  [local(): total = lax.psum(jnp.sum(vnew * vnew), 'gx')]
    reduce_scatter x1 -> x0, local copies, waits for them, and re-layouts: 11.4 us -> none  [local(): lax.psum_scatter(partial_y.astype(jnp.bfloat16), 'gz', scatter_dimension=...]
  transfers between devices with their start and end apart: 4 -> 0, of which waited for: 4 -> 0; matrix products, arithmetic and copies ran while one was open for 0% -> 0% of each run, Pallas kernels for 0% -> 0%
where the time goes in v1:
time: 105 us
  Pallas kernels  103 us (98%)
  local copies, waits for them, and re-layouts  1.57 us (1%)
    pallas_call x1, Pallas kernels, fused(): pl.pallas_call(functools.partial(sweep_kernel, nx, order), out_shape=jax....  103 us

profile of v1, /device:TPU:0, one launch (start us, length us, event | category | flops | bytes accessed | tf_op | source)
XLA Modules:
  0.0 104.9 jit_solution(3858453048892046151)
XLA Ops:
  0.0 103.3 %shard_map.28 = f32[256,128]{1,0:T(8,128)} custom-call(bf16[256,256,512]{2,1,0:T(8,128)(2,1)} %m_hbm.1, bf16[1024,128]{1,0:T(8,128)(2,1)} %u_ref.1), custom_call_target="tpu_custom_call" | custom-call | flops 10737418240 | bytes 67108864 | tf_op jit(solution)/shard_map/pallas_call | solution.py:329
  103.3 1.6 %copy.4 = f32[256,128]{1,0:T(8,128)} copy(f32[256,128]{1,0:T(8,128)} %shard_map.28) | data formatting | bytes 262144

commit v2 on v1

--- a/solution.py
+++ b/solution.py
@@ -12,10 +12,12 @@
 BF16 = jnp.bfloat16
 STEP_ROWS = 16
 MBUFS = 4
-PIECES = 4
-
-
-def sweep_kernel(nx, order, m_hbm, u_ref, out_ref, mbuf, uj_t, ui_t, zf, zsend, prx, kept, xs, rx, zz,
+PIECES = 8
+LAG = 4
+AHEAD = 2
+
+
+def sweep_kernel(nx, order, m_hbm, u_ref, out_ref, mbuf, vs_t, uj_t, ui_t, zown, zsend, prx, xs, ys, rxx, rxy, zz,
                  cs, crx, cown, lsend, r1, r2, cfull, vs, vrx, vfull, ss, ssrx,
                  m_sem, p_send, p_recv, x_send, x_recv, y_send, y_recv, c_send, c_recv, l_send, r1_recv, r2_recv,
                  o_send, g_send, g_recv, v_send, v_recv, f_send, f_recv, s_send, s_recv):
@@ -33,7 +35,7 @@
     quarter = rank // 4
     part = rank // 8
     sub = rank // 16
-    piece = sub // 2
+    piece = 2 * sub // PIECES
 
     def group(d):
         e = lax.rem(me_e + d, 8)
@@ -59,7 +61,12 @@
     for d in range(1, nx):
         pl.semaphore_signal(barrier, inc=1, device_id=line(d), device_id_type=MESH)
 
-    uj_t[...] = u_ref[pl.ds(me_y * rows_j, rows_j), :].astype(F32).T.astype(BF16)
+    uj = u_ref[pl.ds(me_y * rows_j, rows_j), :].astype(F32).T
+    vs_t[...] = uj.astype(BF16)
+    for n, core in enumerate((me_c, 1 - me_c)):
+        for m, first in enumerate((bit_x * part, quarter + bit_y * part,
+                                   (1 - bit_x) * part, quarter + (1 - bit_y) * part)):
+            uj_t[pl.ds(n * half + m * part, part), :] = vs_t[pl.ds(core * half + first, part), :]
     ui_t[...] = u_ref[pl.ds(me_x * rows_i, rows_i), :].astype(F32).T.astype(BF16)
     pl.semaphore_wait(barrier, 7 + nx - 1)
 
@@ -67,13 +74,12 @@
         return remote(zsend.at[t], prx.at[t], p_send.at[t], p_recv.at[t], at_c)
 
     def x_copy(t):
-        return remote(xs.at[t, pl.ds(0, part)], rx.at[t, pl.ds(0, part)], x_send.at[t], x_recv.at[t], at_x)
+        return remote(xs.at[t], rxx.at[t], x_send.at[t], x_recv.at[t], at_x)
 
     def y_copy(t):
-        return remote(xs.at[t, pl.ds(part, part)], rx.at[t, pl.ds(part, part)], y_send.at[t], y_recv.at[t], at_y)
+        return remote(ys.at[t], rxy.at[t], y_send.at[t], y_recv.at[t], at_y)
 
     def contract(t):
-        par = lax.rem(t, 2)
         m_copy(t).wait()
         block = mbuf[lax.rem(t, MBUFS)].reshape(STEP_ROWS * rows_j, rows_k)
         uk = u_ref[pl.ds(me_c * rows_k, rows_k), :]
@@ -81,53 +87,54 @@
         for i in range(0, STEP_ROWS, 2):
             pair = jnp.concatenate([y[i * rows_j:(i + 1) * rows_j], y[(i + 1) * rows_j:(i + 2) * rows_j]], axis=1)
             z = jnp.dot(uj_t[...], pair, preferred_element_type=F32) * scale
-            zf[par, pl.ds(i, rank, stride=STEP_ROWS), :] = z[:, :rank]
-            zf[par, pl.ds(i + 1, rank, stride=STEP_ROWS), :] = z[:, rank:]
-        other = zf[par, pl.ds((1 - me_c) * half * STEP_ROWS, half * STEP_ROWS), :]
-        zsend[t] = other.astype(BF16).reshape(half, STEP_ROWS, rank)
+            for n in range(2):
+                zown[t, i + n] = z[:half, n * rank:(n + 1) * rank]
+                zsend[t, i + n] = z[half:, n * rank:(n + 1) * rank].astype(BF16)
         p_copy(t).start()
 
     def pair_sum(t):
-        par = lax.rem(t, 2)
         p_copy(t).wait_recv()
-
-        def summed(first):
-            mine = zf[par, pl.ds((me_c * half + first) * STEP_ROWS, part * STEP_ROWS), :]
-            return mine.reshape(part, STEP_ROWS, rank) + prx[t, pl.ds(first, part)].astype(F32)
-
-        xs[t, pl.ds(0, part)] = summed((1 - bit_x) * part).astype(BF16)
+        xs[t] = (zown[t, :, pl.ds(2 * part, part)] + prx[t, :, pl.ds(2 * part, part)].astype(F32)).astype(BF16)
         x_copy(t).start()
-        xs[t, pl.ds(part, part)] = summed(quarter + (1 - bit_y) * part).astype(BF16)
+        ys[t] = (zown[t, :, pl.ds(3 * part, part)] + prx[t, :, pl.ds(3 * part, part)].astype(F32)).astype(BF16)
         y_copy(t).start()
-        kept[t, pl.ds(0, part)] = summed(bit_x * part)
-        kept[t, pl.ds(part, part)] = summed(quarter + bit_y * part)
-
-    contract(0)
-
-    def body(t, carry):
+
+    def land(t):
+        x_copy(t).wait_recv()
+        y_copy(t).wait_recv()
+        for i in range(STEP_ROWS):
+            both = zown[t, i, pl.ds(0, 2 * part)] + prx[t, i, pl.ds(0, 2 * part)].astype(F32)
+            far = jnp.concatenate([rxx[t, i], rxy[t, i]], axis=0).astype(F32)
+            zz[pl.ds(t * STEP_ROWS + i, 2 * part, stride=rows_i), :] = both + far
+
+    def fetch(t):
         @pl.when(t + MBUFS - 2 < steps)
         def _():
             m_copy(t + MBUFS - 2).start()
 
+    def early(t, carry):
+        fetch(t)
         pair_sum(t - 1)
         contract(t)
         return carry
 
-    lax.fori_loop(1, steps, body, 0)
+    def body(t, carry):
+        fetch(t)
+        pair_sum(t - 1)
+        land(t - LAG)
+        contract(t)
+        return carry
+
+    contract(0)
+    lax.fori_loop(1, LAG, early, 0)
+    lax.fori_loop(LAG, steps, body, 0)
     pair_sum(steps - 1)
 
-    def landed(t, carry):
-        x_copy(t).wait_recv()
-        y_copy(t).wait_recv()
+    def late(t, carry):
+        land(t)
         return carry
 
-    lax.fori_loop(0, steps, landed, 0)
-
-    def total_z(a, carry):
-        zz[a] = (kept[:, a] + rx[:, a].astype(F32)).astype(BF16).reshape(rows_i, rank)
-        return carry
-
-    lax.fori_loop(0, 2 * part, total_z, 0)
+    lax.fori_loop(steps - LAG, steps, late, 0)
 
     def first_of(k, mine):
         if k % 2 == 0:
@@ -137,7 +144,7 @@
         return part + bit * sub + (k // 2) * piece
 
     def wide_z(first):
-        return jnp.concatenate([zz[first + n] for n in range(piece)], axis=1)
+        return jnp.concatenate([zz[pl.ds((first + n) * rows_i, rows_i), :].astype(BF16) for n in range(piece)], axis=1)
 
     def core_part(first):
         return jnp.dot(ui_t[...], wide_z(first), preferred_element_type=F32) * scale
@@ -150,11 +157,6 @@
         for n in range(piece):
             cs[k, n] = c[:, n * rank:(n + 1) * rank].astype(BF16)
         c_copy(k).start()
-    for k in range(PIECES):
-        c = core_part(first_of(k, True))
-        for n in range(piece):
-            cown[k, n] = c[:, n * rank:(n + 1) * rank]
-
     mid = nx // 2
     side = lax.div(me_x, mid)
     inward = (me_x + 1 - 2 * side, me_y, me_c)
@@ -180,9 +182,11 @@
         here = cfull.at[pl.ds(first_of(k, False), piece)]
         return remote(here, here, g_send.at[k], g_recv.at[k], at_y if k % 2 == 0 else at_x)
 
-    for k in range(PIECES):
+    def to_middle(k):
+        c = core_part(first_of(k, True))
         c_copy(k).wait_recv()
-        cown[k] = cown[k] + crx[k].astype(F32)
+        for n in range(piece):
+            cown[k, n] = c[:, n * rank:(n + 1) * rank] + crx[k, n].astype(F32)
 
         @pl.when(has_out)
         def _():
@@ -203,7 +207,7 @@
         c = jnp.concatenate([cfull[first + n] for n in range(piece)], axis=1)
         return lax.dot_general(wide_z(first), c, (((1,), (1,)), ((), ())), preferred_element_type=F32)
 
-    for k in range(PIECES):
+    def from_middle(k):
         l2_copy(k).wait_recv()
         first = first_of(k, True)
 
@@ -224,6 +228,12 @@
             vs[...] = v_part(first)
         else:
             vs[...] = vs[...] + v_part(first)
+
+    for k in range(PIECES + AHEAD):
+        if k < PIECES:
+            to_middle(k)
+        if k >= AHEAD:
+            from_middle(k - AHEAD)
     for k in range(PIECES):
         g_landed(k).wait_recv()
         vs[...] = vs[...] + v_part(first_of(k, False))
@@ -293,20 +303,22 @@
     rows_i, rows_j, rows_k = moment.shape
     order, rank = factor_start.shape
     steps = rows_i // STEP_ROWS
-    half, part, piece = rank // 2, rank // 8, rank // 32
+    half, part, piece = rank // 2, rank // 8, rank // 64
     vrows = rows_i // 8
     vmem, dma = pltpu.VMEM, pltpu.SemaphoreType.DMA
     scratch = [
         vmem((MBUFS, STEP_ROWS, rows_j, rows_k), BF16),
         vmem((rank, rows_j), BF16),
+        vmem((rank, rows_j), BF16),
         vmem((rank, rows_i), BF16),
-        vmem((2, rank * STEP_ROWS, rank), F32),
-        vmem((steps, half, STEP_ROWS, rank), BF16),
-        vmem((steps, half, STEP_ROWS, rank), BF16),
-        vmem((steps, 2 * part, STEP_ROWS, rank), F32),
-        vmem((steps, 2 * part, STEP_ROWS, rank), BF16),
-        vmem((steps, 2 * part, STEP_ROWS, rank), BF16),
-        vmem((2 * part, rows_i, rank), BF16),
+        vmem((steps, STEP_ROWS, half, rank), F32),
+        vmem((steps, STEP_ROWS, half, rank), BF16),
+        vmem((steps, STEP_ROWS, half, rank), BF16),
+        vmem((steps, STEP_ROWS, part, rank), BF16),
+        vmem((steps, STEP_ROWS, part, rank), BF16),
+        vmem((steps, STEP_ROWS, part, rank), BF16),
+        vmem((steps, STEP_ROWS, part, rank), BF16),
+        vmem((2 * part * rows_i, rank), F32),
         vmem((PIECES, piece, rank, rank), BF16),
         vmem((PIECES, piece, rank, rank), BF16),
         vmem((PIECES, piece, rank, rank), F32),

time: 105 us -> 130 us (1.24)
  Pallas kernels: 103 us -> 128 us
    pallas_call x1, Pallas kernels: 103 us -> 128 us  [fused(): pl.pallas_call(functools.partial(sweep_kernel, nx, order), out_shape=jax....]
where the time goes in v2:
time: 130 us
  Pallas kernels  128 us (98%)
  local copies, waits for them, and re-layouts  1.57 us (1%)
    pallas_call x1, Pallas kernels, fused(): pl.pallas_call(functools.partial(sweep_kernel, nx, order), out_shape=jax....  128 us

profile of v2, /device:TPU:0, one launch (start us, length us, event | category | flops | bytes accessed | tf_op | source)
XLA Modules:
  0.0 129.9 jit_solution(9544330960343590524)
XLA Ops:
  0.0 128.3 %shard_map.28 = f32[256,128]{1,0:T(8,128)} custom-call(bf16[256,256,512]{2,1,0:T(8,128)(2,1)} %m_hbm.1, bf16[1024,128]{1,0:T(8,128)(2,1)} %u_ref.1), custom_call_target="tpu_custom_call" | custom-call | flops 10737418240 | bytes 67108864 | tf_op jit(solution)/shard_map/pallas_call | solution.py:341
  128.3 1.6 %copy.4 = f32[256,128]{1,0:T(8,128)} copy(f32[256,128]{1,0:T(8,128)} %shard_map.28) | data formatting | bytes 262144

commit v3 on v2

--- a/solution.py
+++ b/solution.py
@@ -182,12 +182,13 @@
         here = cfull.at[pl.ds(first_of(k, False), piece)]
         return remote(here, here, g_send.at[k], g_recv.at[k], at_y if k % 2 == 0 else at_x)
 
-    def to_middle(k):
+    def own_sum(k):
         c = core_part(first_of(k, True))
         c_copy(k).wait_recv()
         for n in range(piece):
             cown[k, n] = c[:, n * rank:(n + 1) * rank] + crx[k, n].astype(F32)
 
+    def add_outer(k):
         @pl.when(has_out)
         def _():
             l1_copy(k).wait_recv()
@@ -195,45 +196,47 @@
 
         lsend[k] = cown[k].astype(BF16)
 
-        @pl.when(inner)
-        def _():
-            l2_copy(k).start()
-
-        @pl.when(not_inner)
-        def _():
-            l1_copy(k).start()
-
     def v_part(first):
         c = jnp.concatenate([cfull[first + n] for n in range(piece)], axis=1)
         return lax.dot_general(wide_z(first), c, (((1,), (1,)), ((), ())), preferred_element_type=F32)
 
-    def from_middle(k):
-        l2_copy(k).wait_recv()
-        first = first_of(k, True)
-
-        @pl.when(inner)
-        def _():
-            cfull[pl.ds(first, piece)] = (lsend[k].astype(F32) + r2[k].astype(F32)).astype(BF16)
-
-        @pl.when(not_inner)
-        def _():
-            cfull[pl.ds(first, piece)] = r2[k]
-
+    def send_back(k):
         @pl.when(has_out)
         def _():
             o_copy(k).start()
 
         g_copy(k).start()
-        if k == 0:
-            vs[...] = v_part(first)
-        else:
-            vs[...] = vs[...] + v_part(first)
-
-    for k in range(PIECES + AHEAD):
-        if k < PIECES:
-            to_middle(k)
-        if k >= AHEAD:
-            from_middle(k - AHEAD)
+
+    def add_v(k):
+        part_v = v_part(first_of(k, True))
+        vs[...] = part_v if k == 0 else vs[...] + part_v
+
+    @pl.when(not_inner)
+    def _():
+        for k in range(PIECES):
+            own_sum(k)
+            add_outer(k)
+            l1_copy(k).start()
+        for k in range(PIECES):
+            l2_copy(k).wait_recv()
+            cfull[pl.ds(first_of(k, True), piece)] = r2[k]
+            send_back(k)
+            add_v(k)
+
+    @pl.when(inner)
+    def _():
+        for k in range(PIECES + AHEAD):
+            if k < PIECES:
+                own_sum(k)
+                add_outer(k)
+                l2_copy(k).start()
+            if k >= AHEAD:
+                n = k - AHEAD
+                l2_copy(n).wait_recv()
+                cfull[pl.ds(first_of(n, True), piece)] = (lsend[n].astype(F32) + r2[n].astype(F32)).astype(BF16)
+                send_back(n)
+                add_v(n)
+
     for k in range(PIECES):
         g_landed(k).wait_recv()
         vs[...] = vs[...] + v_part(first_of(k, False))

time: 130 us -> 102 us (0.78)
  Pallas kernels: 128 us -> 99.8 us
    pallas_call x1, Pallas kernels: 128 us -> 99.8 us  [fused(): pl.pallas_call(functools.partial(sweep_kernel, nx, order), out_shape=jax....]
where the time goes in v3:
time: 102 us; the launch traced here: 101 us
  Pallas kernels  99.8 us (98%)
  local copies, waits for them, and re-layouts  1.57 us (2%)
    pallas_call x1, Pallas kernels, fused(): pl.pallas_call(functools.partial(sweep_kernel, nx, order), out_shape=jax....  99.8 us

profile of v3, /device:TPU:0, one launch (start us, length us, event | category | flops | bytes accessed | tf_op | source)
XLA Modules:
  0.0 101.4 jit_solution(7227340579010276843)
XLA Ops:
  0.0 99.8 %shard_map.28 = f32[256,128]{1,0:T(8,128)} custom-call(bf16[256,256,512]{2,1,0:T(8,128)(2,1)} %m_hbm.1, bf16[1024,128]{1,0:T(8,128)(2,1)} %u_ref.1), custom_call_target="tpu_custom_call" | custom-call | flops 10737418240 | bytes 67108864 | tf_op jit(solution)/shard_map/pallas_call | solution.py:344
  99.8 1.6 %copy.4 = f32[256,128]{1,0:T(8,128)} copy(f32[256,128]{1,0:T(8,128)} %shard_map.28) | data formatting | bytes 262144

commit v4 on v3

--- a/solution.py
+++ b/solution.py
@@ -17,7 +17,7 @@
 AHEAD = 2
 
 
-def sweep_kernel(nx, order, m_hbm, u_ref, out_ref, mbuf, vs_t, uj_t, ui_t, zown, zsend, prx, xs, ys, rxx, rxy, zz,
+def sweep_kernel(nx, order, m_hbm, u_ref, out_ref, mbuf, vs_t, uk_t, ui_t, zown, zsend, prx, xs, ys, rxx, rxy, zz,
                  cs, crx, cown, lsend, r1, r2, cfull, vs, vrx, vfull, ss, ssrx,
                  m_sem, p_send, p_recv, x_send, x_recv, y_send, y_recv, c_send, c_recv, l_send, r1_recv, r2_recv,
                  o_send, g_send, g_recv, v_send, v_recv, f_send, f_recv, s_send, s_recv):
@@ -61,12 +61,11 @@
     for d in range(1, nx):
         pl.semaphore_signal(barrier, inc=1, device_id=line(d), device_id_type=MESH)
 
-    uj = u_ref[pl.ds(me_y * rows_j, rows_j), :].astype(F32).T
-    vs_t[...] = uj.astype(BF16)
+    vs_t[...] = u_ref[pl.ds(me_c * rows_k, rows_k), :].astype(F32).T.astype(BF16)
     for n, core in enumerate((me_c, 1 - me_c)):
         for m, first in enumerate((bit_x * part, quarter + bit_y * part,
                                    (1 - bit_x) * part, quarter + (1 - bit_y) * part)):
-            uj_t[pl.ds(n * half + m * part, part), :] = vs_t[pl.ds(core * half + first, part), :]
+            uk_t[pl.ds(n * half + m * part, part), :] = vs_t[pl.ds(core * half + first, part), :]
     ui_t[...] = u_ref[pl.ds(me_x * rows_i, rows_i), :].astype(F32).T.astype(BF16)
     pl.semaphore_wait(barrier, 7 + nx - 1)
 
@@ -80,33 +79,35 @@
         return remote(ys.at[t], rxy.at[t], y_send.at[t], y_recv.at[t], at_y)
 
     def contract(t):
-        m_copy(t).wait()
-        block = mbuf[lax.rem(t, MBUFS)].reshape(STEP_ROWS * rows_j, rows_k)
-        uk = u_ref[pl.ds(me_c * rows_k, rows_k), :]
-        y = jnp.dot(block, uk, preferred_element_type=F32).astype(BF16)
-        for i in range(0, STEP_ROWS, 2):
-            pair = jnp.concatenate([y[i * rows_j:(i + 1) * rows_j], y[(i + 1) * rows_j:(i + 2) * rows_j]], axis=1)
-            z = jnp.dot(uj_t[...], pair, preferred_element_type=F32) * scale
-            for n in range(2):
-                zown[t, i + n] = z[:half, n * rank:(n + 1) * rank]
-                zsend[t, i + n] = z[half:, n * rank:(n + 1) * rank].astype(BF16)
-        p_copy(t).start()
+        uj = u_ref[pl.ds(me_y * rows_j, rows_j), :]
+        slot = lax.rem(t, MBUFS)
+        for i in range(STEP_ROWS):
+            y = lax.dot_general(uk_t[...], mbuf[slot, i], (((1,), (1,)), ((), ())), preferred_element_type=F32)
+            z = jnp.dot(y.astype(BF16), uj, preferred_element_type=F32) * scale
+            zown[t, i] = z[:half]
+            zsend[t, i] = z[half:].astype(BF16)
 
     def pair_sum(t):
-        p_copy(t).wait_recv()
         xs[t] = (zown[t, :, pl.ds(2 * part, part)] + prx[t, :, pl.ds(2 * part, part)].astype(F32)).astype(BF16)
-        x_copy(t).start()
         ys[t] = (zown[t, :, pl.ds(3 * part, part)] + prx[t, :, pl.ds(3 * part, part)].astype(F32)).astype(BF16)
-        y_copy(t).start()
 
     def land(t):
-        x_copy(t).wait_recv()
-        y_copy(t).wait_recv()
         for i in range(STEP_ROWS):
             both = zown[t, i, pl.ds(0, 2 * part)] + prx[t, i, pl.ds(0, 2 * part)].astype(F32)
             far = jnp.concatenate([rxx[t, i], rxy[t, i]], axis=0).astype(F32)
             zz[pl.ds(t * STEP_ROWS + i, 2 * part, stride=rows_i), :] = both + far
 
+    def await_pair(t):
+        p_copy(t).wait_recv()
+
+    def await_far(t):
+        x_copy(t).wait_recv()
+        y_copy(t).wait_recv()
+
+    def send_far(t):
+        x_copy(t).start()
+        y_copy(t).start()
+
     def fetch(t):
         @pl.when(t + MBUFS - 2 < steps)
         def _():
@@ -114,23 +115,37 @@
 
     def early(t, carry):
         fetch(t)
+        await_pair(t - 1)
+        m_copy(t).wait()
         pair_sum(t - 1)
+        send_far(t - 1)
         contract(t)
+        p_copy(t).start()
         return carry
 
     def body(t, carry):
         fetch(t)
+        await_pair(t - 1)
+        await_far(t - LAG)
+        m_copy(t).wait()
         pair_sum(t - 1)
+        send_far(t - 1)
         land(t - LAG)
         contract(t)
+        p_copy(t).start()
         return carry
 
+    m_copy(0).wait()
     contract(0)
+    p_copy(0).start()
     lax.fori_loop(1, LAG, early, 0)
     lax.fori_loop(LAG, steps, body, 0)
+    await_pair(steps - 1)
     pair_sum(steps - 1)
+    send_far(steps - 1)
 
     def late(t, carry):
+        await_far(t)
         land(t)
         return carry
 
@@ -311,8 +326,8 @@
     vmem, dma = pltpu.VMEM, pltpu.SemaphoreType.DMA
     scratch = [
         vmem((MBUFS, STEP_ROWS, rows_j, rows_k), BF16),
-        vmem((rank, rows_j), BF16),
-        vmem((rank, rows_j), BF16),
+        vmem((rank, rows_k), BF16),
+        vmem((rank, rows_k), BF16),
         vmem((rank, rows_i), BF16),
         vmem((steps, STEP_ROWS, half, rank), F32),
         vmem((steps, STEP_ROWS, half, rank), BF16),

time: 102 us -> 143 us (1.40)
  Pallas kernels: 99.8 us -> 142 us
    pallas_call x1, Pallas kernels: 99.8 us -> 142 us  [fused(): pl.pallas_call(functools.partial(sweep_kernel, nx, order), out_shape=jax....]
where the time goes in v4:
time: 143 us
  Pallas kernels  142 us (99%)
  local copies, waits for them, and re-layouts  1.57 us (1%)
    pallas_call x1, Pallas kernels, fused(): pl.pallas_call(functools.partial(sweep_kernel, nx, order), out_shape=jax....  142 us

profile of v4, /device:TPU:0, one launch (start us, length us, event | category | flops | bytes accessed | tf_op | source)
XLA Modules:
  0.0 143.2 jit_solution(16354609587943889321)
XLA Ops:
  0.0 141.6 %shard_map.28 = f32[256,128]{1,0:T(8,128)} custom-call(bf16[256,256,512]{2,1,0:T(8,128)(2,1)} %m_hbm.1, bf16[1024,128]{1,0:T(8,128)(2,1)} %u_ref.1), custom_call_target="tpu_custom_call" | custom-call | flops 10737418240 | bytes 67108864 | tf_op jit(solution)/shard_map/pallas_call | solution.py:359
  141.6 1.6 %copy.4 = f32[256,128]{1,0:T(8,128)} copy(f32[256,128]{1,0:T(8,128)} %shard_map.28) | data formatting | bytes 262144

commit v5 on v3

--- a/solution.py
+++ b/solution.py
@@ -13,11 +13,11 @@
 STEP_ROWS = 16
 MBUFS = 4
 PIECES = 8
-LAG = 4
+LAG = 2
 AHEAD = 2
 
 
-def sweep_kernel(nx, order, m_hbm, u_ref, out_ref, mbuf, vs_t, uj_t, ui_t, zown, zsend, prx, xs, ys, rxx, rxy, zz,
+def sweep_kernel(nx, order, m_hbm, u_ref, out_ref, mbuf, y_even, y_odd, vs_t, uj_t, ui_t, zown, zsend, prx, xs, ys, rxx, rxy, zz,
                  cs, crx, cown, lsend, r1, r2, cfull, vs, vrx, vfull, ss, ssrx,
                  m_sem, p_send, p_recv, x_send, x_recv, y_send, y_recv, c_send, c_recv, l_send, r1_recv, r2_recv,
                  o_send, g_send, g_recv, v_send, v_recv, f_send, f_recv, s_send, s_recv):
@@ -79,62 +79,84 @@
     def y_copy(t):
         return remote(ys.at[t], rxy.at[t], y_send.at[t], y_recv.at[t], at_y)
 
-    def contract(t):
-        m_copy(t).wait()
-        block = mbuf[lax.rem(t, MBUFS)].reshape(STEP_ROWS * rows_j, rows_k)
+    def first_product(t, y_ref):
         uk = u_ref[pl.ds(me_c * rows_k, rows_k), :]
-        y = jnp.dot(block, uk, preferred_element_type=F32).astype(BF16)
-        for i in range(0, STEP_ROWS, 2):
-            pair = jnp.concatenate([y[i * rows_j:(i + 1) * rows_j], y[(i + 1) * rows_j:(i + 2) * rows_j]], axis=1)
-            z = jnp.dot(uj_t[...], pair, preferred_element_type=F32) * scale
-            for n in range(2):
+        slot = lax.rem(t, MBUFS)
+        for i in range(0, STEP_ROWS, 4):
+            block = mbuf[slot, pl.ds(i, 4)].reshape(4 * rows_j, rows_k)
+            y = jnp.dot(block, uk, preferred_element_type=F32)
+            y_ref[pl.ds(i * rows_j, 4 * rows_j), :] = y.astype(BF16)
+
+    def second_product(t, y_ref):
+        for i in range(0, STEP_ROWS, 4):
+            wide = jnp.concatenate([y_ref[pl.ds((i + n) * rows_j, rows_j), :] for n in range(4)], axis=1)
+            z = jnp.dot(uj_t[...], wide, preferred_element_type=F32) * scale
+            for n in range(4):
                 zown[t, i + n] = z[:half, n * rank:(n + 1) * rank]
                 zsend[t, i + n] = z[half:, n * rank:(n + 1) * rank].astype(BF16)
-        p_copy(t).start()
 
     def pair_sum(t):
-        p_copy(t).wait_recv()
         xs[t] = (zown[t, :, pl.ds(2 * part, part)] + prx[t, :, pl.ds(2 * part, part)].astype(F32)).astype(BF16)
-        x_copy(t).start()
         ys[t] = (zown[t, :, pl.ds(3 * part, part)] + prx[t, :, pl.ds(3 * part, part)].astype(F32)).astype(BF16)
-        y_copy(t).start()
 
     def land(t):
-        x_copy(t).wait_recv()
-        y_copy(t).wait_recv()
         for i in range(STEP_ROWS):
             both = zown[t, i, pl.ds(0, 2 * part)] + prx[t, i, pl.ds(0, 2 * part)].astype(F32)
             far = jnp.concatenate([rxx[t, i], rxy[t, i]], axis=0).astype(F32)
             zz[pl.ds(t * STEP_ROWS + i, 2 * part, stride=rows_i), :] = both + far
 
-    def fetch(t):
+    def await_far(t):
+        x_copy(t).wait_recv()
+        y_copy(t).wait_recv()
+
+    def send_far(t):
+        x_copy(t).start()
+        y_copy(t).start()
+
+    def step(t, y_old, y_new, sums, lands):
         @pl.when(t + MBUFS - 2 < steps)
         def _():
             m_copy(t + MBUFS - 2).start()
 
-    def early(t, carry):
-        fetch(t)
-        pair_sum(t - 1)
-        contract(t)
+        if sums:
+            p_copy(t - 2).wait_recv()
+        if lands:
+            await_far(t - 2 - LAG)
+        m_copy(t).wait()
+        if sums:
+            pair_sum(t - 2)
+            send_far(t - 2)
+        if lands:
+            land(t - 2 - LAG)
+        second_product(t - 1, y_old)
+        first_product(t, y_new)
+        p_copy(t - 1).start()
+
+    m_copy(0).wait()
+    first_product(0, y_even)
+    for t in range(1, 2 + LAG):
+        old, new = (y_even, y_odd) if t % 2 else (y_odd, y_even)
+        step(t, old, new, t >= 2, False)
+
+    def body(n, carry):
+        step(2 * n, y_odd, y_even, True, True)
+        step(2 * n + 1, y_even, y_odd, True, True)
         return carry
 
-    def body(t, carry):
-        fetch(t)
-        pair_sum(t - 1)
-        land(t - LAG)
-        contract(t)
-        return carry
-
-    contract(0)
-    lax.fori_loop(1, LAG, early, 0)
-    lax.fori_loop(LAG, steps, body, 0)
-    pair_sum(steps - 1)
+    lax.fori_loop((2 + LAG) // 2, steps // 2, body, 0)
+    second_product(steps - 1, y_odd)
+    p_copy(steps - 1).start()
+    for t in (steps - 2, steps - 1):
+        p_copy(t).wait_recv()
+        pair_sum(t)
+        send_far(t)
 
     def late(t, carry):
+        await_far(t)
         land(t)
         return carry
 
-    lax.fori_loop(steps - LAG, steps, late, 0)
+    lax.fori_loop(steps - 2 - LAG, steps, late, 0)
 
     def first_of(k, mine):
         if k % 2 == 0:
@@ -311,6 +333,8 @@
     vmem, dma = pltpu.VMEM, pltpu.SemaphoreType.DMA
     scratch = [
         vmem((MBUFS, STEP_ROWS, rows_j, rows_k), BF16),
+        vmem((STEP_ROWS * rows_j, rank), BF16),
+        vmem((STEP_ROWS * rows_j, rank), BF16),
         vmem((rank, rows_j), BF16),
         vmem((rank, rows_j), BF16),
         vmem((rank, rows_i), BF16),

time: 102 us -> 99.7 us (0.977)
  Pallas kernels: 99.8 us -> 97.9 us
    pallas_call x1, Pallas kernels: 99.8 us -> 97.9 us  [fused(): pl.pallas_call(functools.partial(sweep_kernel, nx, order), out_shape=jax....]
where the time goes in v5:
time: 99.7 us; the launch traced here: 99.5 us
  Pallas kernels  97.9 us (98%)
  local copies, waits for them, and re-layouts  1.57 us (2%)
    pallas_call x1, Pallas kernels, fused(): pl.pallas_call(functools.partial(sweep_kernel, nx, order), out_shape=jax....  97.9 us

profile of v5, /device:TPU:0, one launch (start us, length us, event | category | flops | bytes accessed | tf_op | source)
XLA Modules:
  0.0 99.5 jit_solution(15016641168756400989)
XLA Ops:
  0.0 97.9 %shard_map.28 = f32[256,128]{1,0:T(8,128)} custom-call(bf16[256,256,512]{2,1,0:T(8,128)(2,1)} %m_hbm.1, bf16[1024,128]{1,0:T(8,128)(2,1)} %u_ref.1), custom_call_target="tpu_custom_call" | custom-call | flops 10737418240 | bytes 67108864 | tf_op jit(solution)/shard_map/pallas_call | solution.py:368
  98.0 1.6 %copy.4 = f32[256,128]{1,0:T(8,128)} copy(f32[256,128]{1,0:T(8,128)} %shard_map.28) | data formatting | bytes 262144

commit v6 on v5

--- a/solution.py
+++ b/solution.py
@@ -82,10 +82,8 @@
     def first_product(t, y_ref):
         uk = u_ref[pl.ds(me_c * rows_k, rows_k), :]
         slot = lax.rem(t, MBUFS)
-        for i in range(0, STEP_ROWS, 4):
-            block = mbuf[slot, pl.ds(i, 4)].reshape(4 * rows_j, rows_k)
-            y = jnp.dot(block, uk, preferred_element_type=F32)
-            y_ref[pl.ds(i * rows_j, 4 * rows_j), :] = y.astype(BF16)
+        block = mbuf[slot].reshape(STEP_ROWS * rows_j, rows_k)
+        y_ref[...] = jnp.dot(block, uk, preferred_element_type=F32).astype(BF16)
 
     def second_product(t, y_ref):
         for i in range(0, STEP_ROWS, 4):

time: 99.7 us -> 117 us (1.17)
  Pallas kernels: 97.9 us -> 115 us
    pallas_call x1, Pallas kernels: 97.9 us -> 115 us  [fused(): pl.pallas_call(functools.partial(sweep_kernel, nx, order), out_shape=jax....]
where the time goes in v6:
time: 117 us
  Pallas kernels  115 us (98%)
  local copies, waits for them, and re-layouts  1.57 us (1%)
    pallas_call x1, Pallas kernels, fused(): pl.pallas_call(functools.partial(sweep_kernel, nx, order), out_shape=jax....  115 us

profile of v6, /device:TPU:0, one launch (start us, length us, event | category | flops | bytes accessed | tf_op | source)
XLA Modules:
  0.0 117.1 jit_solution(5425032348397569635)
XLA Ops:
  0.0 115.5 %shard_map.28 = f32[256,128]{1,0:T(8,128)} custom-call(bf16[256,256,512]{2,1,0:T(8,128)(2,1)} %m_hbm.1, bf16[1024,128]{1,0:T(8,128)(2,1)} %u_ref.1), custom_call_target="tpu_custom_call" | custom-call | flops 10737418240 | bytes 67108864 | tf_op jit(solution)/shard_map/pallas_call | solution.py:366
  115.5 1.6 %copy.4 = f32[256,128]{1,0:T(8,128)} copy(f32[256,128]{1,0:T(8,128)} %shard_map.28) | data formatting | bytes 262144
